TPU v7x, 256 devices: a whole 4x4x8 slice. The times are simulated.
256 devices in a mesh: tile: 64 (over z_lo, y, x, core), chol: 4 (over z_hi).
Axes of the slice: x: 4, y: 4, z: 8 (z_hi: 4, z_lo: 2; z = z_hi * 2 + z_lo), core: 2. Of those that a mesh axis runs over, the one named last changes fastest.
Arguments:
- chol_a: bfloat16 [4096, 64, 1024], P('chol', None, 'tile'), may hold values from -6 to 6
- chol_b: bfloat16 [4096, 4, 1024], P('chol', None, 'tile'), may hold values from -0.09375 to 0.09375
- amplitudes: bfloat16 [256, 1024, 1024], P(None, 'tile'), may hold values from -0.015625 to 0.015625
- virt_irrep: int32 [64], replicated, may hold values from 0 to 7
- pair_irrep: int32 [256], replicated, may hold values from 0 to 7
Outputs:
- ladder: float32 [256, 256], P('tile')
All inputs are finite; a program needn't handle non-finite values.
Results may differ from a plain program's by a relative error of at most 0.017.
Values may be sent and summed in bfloat16 or wider, within the bound.
A program may use at most 128 MiB of HBM per device.

v0:
```python
import jax
import jax.numpy as jnp
from jax import lax
from jax.sharding import PartitionSpec as P

VBLK = 16


def orbital_labels(virt_irrep, virt_count):
    blocks = jnp.arange(virt_count, dtype=jnp.int32) // VBLK
    table = jnp.arange(virt_irrep.shape[0], dtype=jnp.int32)
    picks = (blocks[:, None] == table[None, :]).astype(jnp.int32)
    return jnp.sum(picks * virt_irrep[None, :], axis=1)


def ladder_fold(left_rows, columns, column_labels, row_labels, pair_irrep, a_rows, b_rows):
    pair_count, c_rows = (columns.shape[0], columns.shape[1])

    def accumulate(running, vectors, offset):
        vec_count, col_count = (vectors.shape[0], vectors.shape[2])
        factor = vectors.reshape(vec_count, b_rows * col_count)
        integral = lax.dot_general(
            left_rows, factor, (((0,), (0,)), ((), ())), preferred_element_type=jnp.float32
        )
        integral = integral.astype(jnp.bfloat16).reshape(a_rows, c_rows, b_rows, col_count)
        allowed = (
            jnp.bitwise_xor(row_labels[:, None], column_labels[None, :])[None, :, :]
            == pair_irrep[:, None, None]
        )
        masked = jnp.where(allowed, columns, jnp.zeros_like(columns))
        update = jnp.einsum("icd,acbd->iab", masked, integral, preferred_element_type=jnp.float32)
        return update.reshape(pair_count, a_rows * b_rows)

    return accumulate


def body(chol_a, chol_b, amplitudes, virt_irrep, pair_irrep):
    vec_local, a_rows, c_rows = chol_a.shape
    b_rows = chol_b.shape[1]
    pair_count = amplitudes.shape[0]
    virt_count = amplitudes.shape[2]
    labels_all = orbital_labels(virt_irrep, virt_count)
    row_labels = lax.dynamic_slice_in_dim(labels_all, lax.axis_index("tile") * c_rows, c_rows, 0)
    initial = jnp.zeros((pair_count, a_rows * b_rows), jnp.float32)
    left_rows = chol_a.reshape(vec_local, a_rows * c_rows)
    accumulate = ladder_fold(
        left_rows, amplitudes, labels_all, row_labels, pair_irrep, a_rows, b_rows
    )
    partial_value = accumulate(
        initial, lax.all_gather(chol_b, "tile", axis=2, tiled=True), jnp.int32(0)
    )
    summed = lax.psum(partial_value.astype(jnp.bfloat16), "chol").astype(jnp.float32)
    return lax.psum_scatter(summed, "tile", scatter_dimension=0, tiled=True)


def solution(mesh):
    placed = (P("chol", None, "tile"), P("chol", None, "tile"), P(None, "tile", None), P(), P())
    return jax.shard_map(
        body, mesh=mesh, in_specs=placed, out_specs=P("tile", None), check_vma=False
    )
```

profile of v0, /device:TPU:1, one launch (start us, length us, event | category | flops | bytes accessed | tf_op | source)
XLA Modules:
  0.0 520.8 jit_solution(3928692865213655705)
XLA Ops:
  6.5 0.0 copy-start
  6.5 0.0 all-gather.2.cloned.1.call-start
  6.5 0.7 all-gather.2.cloned.1.call-update
  7.3 0.0 all-reduce.4.cloned.1.call-start
  7.3 0.8 select_reduce_fusion
  8.1 0.1 dynamic_slice.3
  8.2 0.1 broadcast_xor_fusion
  8.2 7.9 %compare_select_fusion = bf16[256,16,1024]{2,1,0:T(8,128)(2,1)} fusion(bf16[256,16,1024]{2,1,0:T(8,128)(2,1)} %param.7, s32[16,1024]{1,0:T(8,128)S(1)} %broadcast_xor_fusion, s32[256]{0:T(256)} %param.9), kind=kLoop, calls=%fused_computation | loop fusion | flops 8388608 | bytes 16843776 | tf_op jit(solution)/shard_map/jit(_where)/select_n | solution.py:30
  16.1 110.9 %all-gather.2.cloned.1.call-done = bf16[1024,4,1024]{0,2,1:T(8,128)(2,1)} async-done(((bf16[1024,4,16]{0,2,1:T(8,128)(2,1)}), bf16[1024,4,1024]{0,2,1:T(8,128)(2,1)}) %all-gather.2.cloned.1.call-update) | async-done | bytes 8388624 | tf_op jit(solution)/shard_map/all_gather | solution.py:50
  127.0 0.0 copy-done
  127.0 14.3 %convolution_convert_fusion = bf16[1024,4096]{1,0:T(8,128)(2,1)} fusion(bf16[1024,1024]{0,1:T(8,128)(2,1)S(1)} %bitcast.13, bf16[1024,4096]{0,1:T(8,128)(2,1)} %bitcast.15), kind=kOutput, calls=%fused_computation.3 | convolution fusion | flops 8594128896 | bytes 18874368 | tf_op jit(solution)/shard_map/dot_general | solution.py:22
  141.3 14.6 %reshape.55 = bf16[64,16,4,1024]{3,2,1,0:T(4,128)(2,1)} reshape(bf16[1024,4096]{1,0:T(8,128)(2,1)} %convolution_convert_fusion) | data formatting | bytes 16777216 | tf_op jit(solution)/shard_map/reshape | solution.py:25
  155.9 8.1 %copy.10 = bf16[64,4,16,1024]{3,1,0,2:T(4,128)(2,1)} copy(bf16[64,4,16,1024]{3,1,2,0:T(4,128)(2,1)} %bitcast.14) | data formatting | bytes 16777216 | tf_op jit(solution)/shard_map/icd,acbd->iab/dot_general | solution.py:31
  164.0 12.5 %dot_general.12 = bf16[256,16,1024]{2,0,1:T(8,128)(2,1)} reshape(bf16[64,4,16,1024]{3,1,0,2:T(4,128)(2,1)} %copy.10) | data formatting | bytes 16777216 | tf_op jit(solution)/shard_map/icd,acbd->iab/dot_general | solution.py:31
  176.5 0.0 copy-start.1
  176.5 16.3 %fusion.5 = bf16[256,256]{1,0:T(8,128)(2,1)} fusion(bf16[256,16,1024]{2,0,1:T(8,128)(2,1)} %dot_general.12, bf16[256,16,1024]{2,1,0:T(8,128)(2,1)} %compare_select_fusion), kind=kOutput, calls=%fused_computation.5 | convolution fusion | flops 2147549184 | bytes 16908288 | tf_op jit(solution)/shard_map/icd,acbd->iab/dot_general | solution.py:31
  192.8 0.0 all-reduce.4.cloned.1.call-update
  192.8 0.0 copy-done.1
  192.8 0.6 dynamic-slice
  194.1 45.0 %all-reduce.4.cloned.1.call-done = bf16[256,256]{1,0:T(8,128)(2,1)} async-done(((bf16[256,256]{1,0:T(8,128)(2,1)}), bf16[256,256]{1,0:T(8,128)(2,1)}) %all-reduce.4.cloned.1.call-update) | async-done | bytes 131088 | tf_op jit(solution)/shard_map/psum | solution.py:52
  239.0 274.3 %all-reduce.5 = f32[256,256]{1,0:T(8,128)S(1)} all-reduce(bf16[256,256]{1,0:T(8,128)(2,1)} %all-reduce.4.cloned.1.call-done), channel_id=2, replica_groups=mesh['tile'=64,'chol'=4] {'tile'}, use_global_device_ids=true, to_apply=%region_2.3.clone | all-reduce | flops 65536 | bytes 393216
  513.3 0.6 constant_dynamic-slice_fusion
  (1 shorter events, 0.0 us)
Async XLA Ops:
  6.5 120.5 %copy-start = (bf16[1024,64,16]{0,2,1:T(8,128)(2,1)S(1)}, bf16[1024,64,16]{0,2,1:T(8,128)(2,1)}, u32[]{:S(2)}) copy-start(bf16[1024,64,16]{0,2,1:T(8,128)(2,1)} %param.5) | copy-start | bytes 6291460
  6.5 120.5 %all-gather.2.cloned.1.call-start = ((), (), s32[]{:S(2)}) async-start(), calls=%async_computation | async-start | bytes 8519680 | tf_op jit(solution)/shard_map/all_gather | solution.py:50
  7.3 231.8 %all-reduce.4.cloned.1.call-start = ((), (), s32[]{:S(2)}) async-start(), calls=%async_computation.1 | async-start | bytes 262144 | tf_op jit(solution)/shard_map/psum | solution.py:52
  176.5 16.3 %copy-start.1 = (u32[256]{0:T(256)S(1)}, u32[256]{0:T(256)}, u32[]{:S(2)}) copy-start(u32[256]{0:T(256)} %constant.36) | copy-start | bytes 3076
Sparse Core Ops, SparseCore 0:
  9.2 117.7 all-gather.1
  192.9 46.0 all-reduce.3
where the time goes:
time: 526 us; the launch traced here: 521 us
  blocking collectives  274 us (52%)
  waiting for transfers between devices  157 us (30%)
  local copies, waits for them, and re-layouts  36.5 us (7%)
  matrix products  30.5 us (6%)
  between operations  14.1 us (3%)
  other arithmetic  8.71 us (2%)
    unnamed x1, blocking collectives  274 us
    all_gather x1, waiting for transfers between devices, body(): lax.all_gather(chol_b, 'tile', axis=2, tiled=True)  111 us
    psum x1, waiting for transfers between devices, body(): lax.psum(partial_value.astype(jnp.bfloat16), 'chol').astype(jnp.float32)  45 us
    dot_general x2, local copies, waits for them, and re-layouts, accumulate(): jnp.einsum('icd,acbd->iab', masked, integral, preferred_element_type=jnp....  20.6 us
    dot_general x1, matrix products, accumulate(): jnp.einsum('icd,acbd->iab', masked, integral, preferred_element_type=jnp....  16.3 us
    reshape x1, local copies, waits for them, and re-layouts, accumulate(): integral.astype(jnp.bfloat16).reshape(a_rows, c_rows, b_rows, col_count)  14.6 us
    dot_general x1, matrix products, accumulate(): lax.dot_general(left_rows, factor, (((0,), (0,)), ((), ())), preferred_el...  14.3 us
  transfers between devices with their start and end apart: 2, of which 2 were waited for; matrix products, arithmetic and copies ran while one was open for 2% of the time, Pallas kernels for 0%

commit v1 on v0

v1 whole, which is shorter than its diff:
```python
import jax
import jax.numpy as jnp
from jax import lax
from jax.experimental import pallas as pl
from jax.experimental.pallas import tpu as pltpu
from jax.sharding import PartitionSpec as P

F32, BF16 = jnp.float32, jnp.bfloat16
MESH = pl.DeviceIdType.MESH
NT = (((1,), (1,)), ((), ()))
CHUNKS = 8
PART = {"X": (0, 512), "Y": (512, 512)}
MOVES = [
    ('y+', 'X', 0, 0, 0, None),
    ('y-', 'X', 0, 0, 0, None),
    ('y+', 'X', 0, 3, 0, 0),
    ('y-', 'X', 0, 1, 0, 1),
    ('z', 'X', 0, 0, 0, None),
    ('z', 'X', 0, 1, 0, None),
    ('z', 'X', 0, 3, 0, None),
    ('z', 'X', 0, 2, 0, None),
    ('z', 'X', 0, 0, 1, None),
    ('z', 'X', 0, 0, 3, None),
    ('x+', 'X', 0, 0, 0, None),
    ('x-', 'X', 0, 0, 0, None),
    ('x+', 'X', 0, 1, 0, None),
    ('x-', 'X', 0, 1, 0, None),
    ('x+', 'X', 0, 3, 0, None),
    ('x-', 'X', 0, 3, 0, None),
    ('x+', 'X', 0, 2, 0, None),
    ('x-', 'X', 0, 2, 0, None),
    ('x+', 'X', 1, 1, 0, None),
    ('x-', 'X', 1, 1, 0, None),
    ('x+', 'X', 1, 3, 0, None),
    ('x-', 'X', 1, 3, 0, None),
    ('x+', 'X', 1, 2, 0, None),
    ('x-', 'X', 1, 2, 0, None),
    ('x+', 'X', 0, 0, 3, None),
    ('x-', 'X', 1, 0, 1, None),
    ('x+', 'X', 0, 1, 3, None),
    ('x-', 'X', 1, 1, 1, None),
    ('x+', 'X', 0, 3, 3, None),
    ('x-', 'X', 1, 3, 1, None),
    ('x+', 'X', 0, 2, 3, None),
    ('x-', 'X', 1, 2, 1, None),
    ('x+', 'Y', 0, 0, 0, None),
    ('x-', 'Y', 0, 0, 0, None),
    ('x+', 'Y', 0, 0, 3, 0),
    ('x-', 'Y', 0, 0, 1, 1),
    ('z', 'Y', 0, 0, 0, None),
    ('z', 'Y', 0, 0, 1, None),
    ('z', 'Y', 0, 0, 3, None),
    ('z', 'Y', 0, 0, 2, None),
    ('z', 'Y', 0, 1, 0, None),
    ('z', 'Y', 0, 3, 0, None),
    ('y+', 'Y', 0, 0, 0, None),
    ('y-', 'Y', 0, 0, 0, None),
    ('y+', 'Y', 0, 0, 1, None),
    ('y-', 'Y', 0, 0, 1, None),
    ('y+', 'Y', 0, 0, 3, None),
    ('y-', 'Y', 0, 0, 3, None),
    ('y+', 'Y', 0, 0, 2, None),
    ('y-', 'Y', 0, 0, 2, None),
    ('y+', 'Y', 1, 0, 1, None),
    ('y-', 'Y', 1, 0, 1, None),
    ('y+', 'Y', 1, 0, 3, None),
    ('y-', 'Y', 1, 0, 3, None),
    ('y+', 'Y', 1, 0, 2, None),
    ('y-', 'Y', 1, 0, 2, None),
    ('y+', 'Y', 0, 3, 0, None),
    ('y-', 'Y', 1, 1, 0, None),
    ('y+', 'Y', 0, 3, 1, None),
    ('y-', 'Y', 1, 1, 1, None),
    ('y+', 'Y', 0, 3, 3, None),
    ('y-', 'Y', 1, 1, 3, None),
    ('y+', 'Y', 0, 3, 2, None),
    ('y-', 'Y', 1, 1, 2, None),
    ('c', 'X', 0, 0, None, None),
    ('c', 'Y', 0, 0, None, None),
    ('c', 'X', 1, 0, None, None),
    ('c', 'Y', 1, 0, None, None),
    ('c', 'X', 0, 1, None, None),
    ('c', 'Y', 0, 1, None, None),
    ('c', 'X', 1, 1, None, None),
    ('c', 'Y', 1, 1, None, None),
    ('c', 'X', 0, 3, None, None),
    ('c', 'Y', 0, 3, None, None),
    ('c', 'X', 1, 3, None, None),
    ('c', 'Y', 1, 3, None, None),
    ('c', 'X', 0, 2, None, None),
    ('c', 'Y', 0, 2, None, None),
    ('c', 'X', 1, 2, None, None),
    ('c', 'Y', 1, 2, None, None),
]
BEFORE_LEFT = [
    [],
    [],
    [],
    [],
]
BEFORE_AMPS = [
    [],
    [],
    [],
    [],
    [],
    [],
    [],
    [('barrier', 0), ('send', 1), ('send', 11), ('send', 36), ('send', 42), ('send', 32), ('send', 0), ('send', 10), ('send', 43), ('send', 33), ('send', 4)],
    [],
    [],
    [],
    [],
    [],
    [],
    [],
    [],
]
BEFORE_HALF = [
    [
        [('wait', 1), ('send', 5), ('send', 12), ('send', 3), ('send', 13), ('wait', 11), ('send', 8), ('wait', 36), ('wait', 42), ('send', 56), ('wait', 32), ('send', 47), ('send', 46), ('send', 34), ('send', 38), ('wait', 43), ('wait', 33), ('send', 44), ('send', 35), ('send', 45), ('wait', 4), ('wait', 0), ('send', 14), ('send', 15), ('wait', 10), ('send', 24), ('send', 37), ('send', 2), ('wait', 3), ('wait', 5), ('send', 19), ('send', 18), ('wait', 12), ('wait', 13), ('wait', 56), ('send', 9), ('wait', 34), ('wait', 47), ('wait', 35), ('send', 65), ('send', 49), ('send', 48), ('send', 26), ('wait', 8), ('send', 25), ('wait', 46), ('send', 60), ('send', 39), ('wait', 65), ('wait', 14), ('wait', 45), ('wait', 15), ('send', 28), ('wait', 38), ('send', 52), ('send', 53), ('wait', 44), ('send', 6), ('wait', 24), ('send', 64), ('wait', 19), ('send', 27), ('wait', 2), ('send', 17), ('wait', 49), ('send', 69), ('send', 16), ('send', 58), ('wait', 37), ('send', 51), ('send', 7), ('wait', 64)],
        [('wait', 26), ('send', 68), ('wait', 60), ('wait', 27), ('send', 70), ('wait', 73), ('send', 62), ('wait', 39), ('send', 67), ('send', 55), ('wait', 51), ('send', 59), ('wait', 66), ('send', 41), ('wait', 28), ('send', 72), ('wait', 68), ('wait', 52), ('wait', 17), ('send', 54), ('wait', 70), ('wait', 6), ('send', 21), ('send', 20), ('wait', 67)],
        [],
        [('wait', 62), ('send', 77), ('wait', 71)],
        [('wait', 63), ('wait', 22), ('wait', 76)],
        [('wait', 74), ('wait', 31), ('send', 78)],
        [],
        [],
    ],
    [
        [('wait', 18), ('wait', 25), ('wait', 69), ('wait', 48), ('send', 73), ('send', 50)],
        [('wait', 72), ('wait', 16), ('send', 30), ('wait', 61), ('wait', 58)],
        [('wait', 55), ('send', 63), ('wait', 50), ('wait', 40), ('send', 57), ('send', 71)],
        [('wait', 41), ('wait', 30), ('send', 76), ('wait', 23), ('send', 31)],
        [('wait', 29), ('send', 74), ('wait', 75)],
        [('wait', 79)],
        [],
        [],
    ],
]
BEFORE_FOLD = [
    [('send', 40), ('wait', 9), ('send', 66), ('wait', 53), ('send', 61)],
    [('wait', 7), ('send', 22), ('send', 23)],
    [('wait', 21), ('send', 29), ('wait', 20), ('wait', 59)],
    [('wait', 54), ('send', 75), ('wait', 77)],
    [('wait', 57), ('send', 79)],
    [('wait', 78)],
    [],
    [],
]


class Place:
    def __init__(self):
        self.tile, self.chol = lax.axis_index("tile"), lax.axis_index("chol")
        self.core = lax.rem(self.tile, 2)
        self.x = lax.rem(lax.div(self.tile, 2), 4)
        self.y = lax.rem(lax.div(self.tile, 8), 4)
        self.z = lax.div(self.tile, 32)
        self.xy = self.y * 4 + self.x
        self.slab = self.chol * 2 + self.z

    def device(self, z, y, x, core, chol=None):
        return (((z * 4 + y) * 4 + x) * 2 + core, self.chol if chol is None else chol)

    def neighbour(self, link):
        z, y, x, core = self.z, self.y, self.x, self.core
        if link == "z":
            return self.device(1 - z, y, x, core)
        if link == "c":
            return self.device(z, y, x, 1 - core)
        step = 1 if link[1] == "+" else 3
        if link[0] == "x":
            return self.device(z, y, lax.rem(x + step, 4), core)
        return self.device(z, lax.rem(y + step, 4), x, core)

    def in_plane(self, other):
        return self.device(self.z, lax.div(other, 4), lax.rem(other, 4), self.core)

    def on_column(self, other):
        return self.device(lax.rem(other, 2), self.y, self.x, self.core, lax.div(other, 2))


def region(held, at, part, dz, dy, dx, half, core):
    z, y = lax.rem(at.z + dz, 2), lax.rem(at.y + dy, 4)
    x = slice(None) if dx is None else lax.rem(at.x + dx, 4)
    cols = PART[part]
    rows = slice(None) if half is None else pl.ds(2 * half, 2)
    return held.at[rows, z, y, x, core, :, pl.ds(cols[0], cols[1])]


def received(link, dz, dy, dx):
    if link == "z":
        return 1 - dz, dy, dx
    if link == "c":
        return dz, dy, dx
    step = 3 if link[1] == "+" else 1
    if link[0] == "x":
        return dz, dy, (dx + step) % 4
    return dz, (dy + step) % 4, dx


def transfer(at, held, send_sems, recv_sems, number, incoming):
    link, part, dz, dy, dx, half = MOVES[number]
    core = at.core
    if incoming:
        dz, dy, dx = received(link, dz, dy, dx)
        core = 1 - core if link == "c" else core
    block = region(held, at, part, dz, dy, dx, half, core)
    return pltpu.make_async_remote_copy(
        src_ref=block,
        dst_ref=block,
        send_sem=send_sems.at[number],
        recv_sem=recv_sems.at[number],
        device_id=at.neighbour(link),
        device_id_type=MESH,
    )


def chunk_of(at, step):
    turn = lax.div(step, 2)
    dy = turn + lax.div(turn, 2) - 2 * lax.div(turn, 3)
    return lax.rem(at.z + lax.rem(step, 2), 2), lax.rem(at.y + dy, 4)


def kernel(
    chol_a, chol_b, amps, virt, pair, out,
    held, left, amps_in, amps_c, mask, integral, acc,
    halves, plane_out, plane_in, column_out, column_in, left_in,
    send_sems, recv_sems, load_sems, half_sems, plane_sems, column_sems,
):
    at = Place()
    loads = [
        pltpu.make_async_copy(chol_b, held.at[:, at.z, at.y, at.x, at.core], load_sems.at[0]),
        pltpu.make_async_copy(chol_a, left_in, load_sems.at[1]),
    ]
    for piece in range(8):
        rows = pl.ds((piece // 2 + 4 * (piece % 2)) * 32, 32)
        loads.append(pltpu.make_async_copy(amps.at[rows], amps_in.at[rows], load_sems.at[2 + piece]))
    for load in loads:
        load.start()
    barrier = pltpu.get_barrier_semaphore()
    peers = [at.neighbour("c")]
    peers += [at.in_plane(lax.rem(at.xy + step, 16)) for step in range(1, 16)]
    peers += [at.on_column(lax.rem(at.slab + step, 8)) for step in range(1, 8)]
    for peer in peers:
        pl.semaphore_signal(barrier, inc=1, device_id=peer, device_id_type=MESH)

    def move(kind, number):
        copy = transfer(at, held, send_sems, recv_sems, number, kind == "wait")
        if kind == "send":
            copy.start()
        else:
            copy.wait_recv()

    def moves(table, step):
        for turn, entries in enumerate(table):
            if entries:

                @pl.when(step == turn)
                def _():
                    for kind, number in entries:
                        if kind == "barrier":
                            loads[0].wait()
                            pl.semaphore_wait(barrier, len(peers))
                        else:
                            move(kind, number)

    def iota(shape, dim):
        return lax.broadcasted_iota(jnp.int32, shape, dim)

    virt_row = jnp.broadcast_to(virt[...], (8, 64)).astype(F32).astype(BF16)
    spread = (lax.div(iota((64, 1024), 1), 16) == iota((64, 1024), 0)).astype(F32).astype(BF16)
    own = (iota((64, 1024), 0) == at.tile).astype(F32).astype(BF16)
    label = jnp.dot(virt_row, spread, preferred_element_type=F32).astype(jnp.int32)
    mine = jnp.dot(virt_row, own, preferred_element_type=F32).astype(jnp.int32)
    wanted = jnp.bitwise_xor(label, mine)[:1]
    row = iota((256, 256), 0)
    source = (
        lax.rem(lax.div(row, 4), 2) * 128 + lax.div(row, 16) * 8
        + lax.rem(lax.div(row, 8), 2) * 4 + lax.rem(row, 4)
    )
    order = (iota((256, 256), 1) == source).astype(F32).astype(BF16)
    pair_row = jnp.broadcast_to(pair[...], (128, 256)).astype(F32).astype(BF16)
    pair_col = lax.dot_general(order, pair_row, NT, preferred_element_type=F32).astype(jnp.int32)
    for chunk in range(CHUNKS):
        cols = slice(chunk * 128, (chunk + 1) * 128)
        mask[chunk] = (pair_col == wanted[:, cols]).astype(F32).astype(BF16)
    acc[...] = jnp.zeros_like(acc)

    loads[1].wait()

    @pl.loop(0, 4)
    def _(group):
        moves(BEFORE_LEFT, group)
        rows = pl.ds(pl.multiple_of(group * 16, 16), 16)
        for cols in range(0, 1024, 128):
            block = left_in[rows, :, cols : cols + 128]
            left[:, rows, cols : cols + 128] = jnp.swapaxes(block, 0, 1)

    @pl.loop(0, 16)
    def _(group):
        for piece in range(4):

            @pl.when(group == 4 * piece)
            def _():
                loads[2 + 2 * piece].wait()
                loads[3 + 2 * piece].wait()

        moves(BEFORE_AMPS, group)
        rows = pl.ds(pl.multiple_of(group * 16, 16), 16)
        for chunk in range(CHUNKS):
            cols = slice(chunk * 128, (chunk + 1) * 128)
            block = jnp.concatenate(
                [
                    amps_in[pl.ds(128 * z + group * 8 + 4 * core, 4), :, cols]
                    for core in range(2)
                    for z in range(2)
                ],
                0,
            )
            amps_c[chunk, :, rows, :] = jnp.swapaxes(block, 0, 1) * mask[chunk, rows, :][None]

    @pl.loop(0, CHUNKS)
    def _(step):
        z, y = chunk_of(at, step)
        for half in range(2):
            moves(BEFORE_HALF[half], step)
            vectors = held[2 * half : 2 * half + 2, z, y].reshape(256, 1024)
            block = lax.dot_general(
                left[...].reshape(1024, 1024), vectors, NT, preferred_element_type=F32
            ).astype(BF16)
            for c in range(16):
                for b in range(2):
                    integral[(2 * half + b) * 64 : (2 * half + b + 1) * 64, c * 128 : (c + 1) * 128] = (
                        block[c * 64 : (c + 1) * 64, b * 128 : (b + 1) * 128]
                    )
        moves(BEFORE_FOLD, step)
        masked = jnp.concatenate([amps_c[z * 4 + y, c] for c in range(16)], 1)
        acc[...] += lax.dot_general(
            masked, integral[...], NT, preferred_element_type=F32
        ).reshape(16, 2, 8, 256)

    swap = pltpu.make_async_remote_copy(
        src_ref=acc.at[:, 1 - at.core],
        dst_ref=halves,
        send_sem=half_sems.at[0],
        recv_sem=half_sems.at[1],
        device_id=at.neighbour("c"),
        device_id_type=MESH,
    )
    swap.start()
    turn = (
        (lax.rem(iota((256, 256), 0), 64) == lax.div(iota((256, 256), 1), 4))
        & (lax.div(iota((256, 256), 0), 64) == lax.rem(iota((256, 256), 1), 4))
    ).astype(F32).astype(BF16)
    swap.wait_recv()
    pairs = (acc[:, at.core] + halves[...]).reshape(128, 256).astype(BF16)
    pairs = jnp.dot(pairs, turn, preferred_element_type=F32).reshape(16, 8, 256)
    plane_out[...] = jnp.concatenate([pairs[:, :, :128], pairs[:, :, 128:]], 1).astype(BF16)
    copies = []
    for step in range(1, 16):
        other = lax.rem(at.xy + step, 16)
        copies.append(
            pltpu.make_async_remote_copy(
                src_ref=plane_out.at[other],
                dst_ref=plane_in.at[at.xy],
                send_sem=plane_sems.at[0, other],
                recv_sem=plane_sems.at[1, at.xy],
                device_id=at.in_plane(other),
                device_id_type=MESH,
            )
        )
        copies[-1].start()
    total = plane_out[at.xy].astype(F32)
    for step in range(1, 16):
        other = lax.rem(at.xy + step, 16)
        pltpu.make_async_remote_copy(
            src_ref=plane_out.at[other],
            dst_ref=plane_in.at[other],
            send_sem=plane_sems.at[0, other],
            recv_sem=plane_sems.at[1, other],
            device_id=at.in_plane(other),
            device_id_type=MESH,
        ).wait_recv()
        total += plane_in[other].astype(F32)
    column_out[...] = total.astype(BF16)
    for step in range(1, 8):
        other = lax.rem(at.slab + step, 8)
        copies.append(
            pltpu.make_async_remote_copy(
                src_ref=column_out,
                dst_ref=column_in.at[at.slab],
                send_sem=column_sems.at[0, other],
                recv_sem=column_sems.at[1, at.slab],
                device_id=at.on_column(other),
                device_id_type=MESH,
            )
        )
        copies[-1].start()
    total = column_out[...].astype(F32)
    for step in range(1, 8):
        other = lax.rem(at.slab + step, 8)
        pltpu.make_async_remote_copy(
            src_ref=column_out,
            dst_ref=column_in.at[other],
            send_sem=column_sems.at[0, other],
            recv_sem=column_sems.at[1, other],
            device_id=at.on_column(other),
            device_id_type=MESH,
        ).wait_recv()
        total += column_in[other].astype(F32)
    total = jnp.where(at.z == 0, total.reshape(2, 2, 4, 128)[:, 0], total.reshape(2, 2, 4, 128)[:, 1])
    out[:, :128] = total[0]
    out[:, 128:] = total[1]
    for number in range(len(MOVES)):
        transfer(at, held, send_sems, recv_sems, number, False).wait_send()
    swap.wait_send()
    for copy in copies:
        copy.wait_send()


def body(chol_a, chol_b, amplitudes, virt_irrep, pair_irrep):
    vec, a_rows, c_rows = chol_a.shape
    b_rows = chol_b.shape[1]
    pairs, _, virt = amplitudes.shape
    anywhere = pl.BlockSpec(memory_space=pl.ANY)
    inside = pl.BlockSpec(memory_space=pltpu.VMEM)
    dma = pltpu.SemaphoreType.DMA
    return pl.pallas_call(
        kernel,
        out_shape=jax.ShapeDtypeStruct((4, 256), F32),
        in_specs=[anywhere, anywhere, anywhere, inside, inside],
        out_specs=inside,
        scratch_shapes=[
            pltpu.VMEM((b_rows, 2, 4, 4, 2, 16, vec), BF16),
            pltpu.VMEM((c_rows, a_rows, vec), BF16),
            pltpu.VMEM((pairs, c_rows, virt), BF16),
            pltpu.VMEM((CHUNKS, c_rows, pairs, 128), BF16),
            pltpu.VMEM((CHUNKS, pairs, 128), BF16),
            pltpu.VMEM((256, 2048), BF16),
            pltpu.VMEM((16, 2, 8, 256), F32),
            pltpu.VMEM((16, 8, 256), F32),
            pltpu.VMEM((16, 16, 128), BF16),
            pltpu.VMEM((16, 16, 128), BF16),
            pltpu.VMEM((16, 128), BF16),
            pltpu.VMEM((8, 16, 128), BF16),
            pltpu.VMEM((a_rows, c_rows, vec), BF16),
            dma((len(MOVES),)),
            dma((len(MOVES),)),
            dma((10,)),
            dma((2,)),
            dma((2, 16)),
            dma((2, 8)),
        ],
        compiler_params=pltpu.CompilerParams(
            collective_id=0, has_side_effects=True, vmem_limit_bytes=56 * 2**20
        ),
        name="ladder",
    )(
        jnp.transpose(chol_a, (1, 2, 0)),
        jnp.transpose(chol_b, (1, 2, 0)),
        amplitudes,
        virt_irrep.reshape(1, -1),
        pair_irrep.reshape(1, -1),
    )


def solution(mesh):
    placed = (P("chol", None, "tile"), P("chol", None, "tile"), P(None, "tile", None), P(), P())
    return jax.shard_map(
        body, mesh=mesh, in_specs=placed, out_specs=P("tile", None), check_vma=False
    )
```

time: 526 us -> 66.1 us (0.13)
  blocking collectives: 274 us -> 0 us
  waiting for transfers between devices: 157 us -> 0 us
  Pallas kernels: 0 us -> 64.7 us
  local copies, waits for them, and re-layouts: 36.5 us -> 1.28 us
  matrix products: 30.5 us -> 0 us
  between operations: 14.1 us -> 0.01 us
  other arithmetic: 8.71 us -> 0 us
    unnamed x1 -> x0, blocking collectives: 274 us -> none
    all_gather x1 -> x0, waiting for transfers between devices: 111 us -> none  [body(): lax.all_gather(chol_b, 'tile', axis=2, tiled=True)]
    pallas_call x0 -> x1, Pallas kernels: none -> 64.7 us  [body(): pl.pallas_call(kernel, out_shape=jax.ShapeDtypeStruct((4, 256), F32), in_...]
    psum x1 -> x0, waiting for transfers between devices: 45 us -> none  [body(): lax.psum(partial_value.astype(jnp.bfloat16), 'chol').astype(jnp.float32)]
    dot_general x2 -> x0, matrix products: 30.5 us -> none  [the longest x1 16.3 us: accumulate(): jnp.einsum('icd,acbd->iab', masked, integral, preferred_element_type=jnp....]
    dot_general x2 -> x0, local copies, waits for them, and re-layouts: 20.6 us -> none  [accumulate(): jnp.einsum('icd,acbd->iab', masked, integral, preferred_element_type=jnp....]
    reshape x1 -> x0, local copies, waits for them, and re-layouts: 14.6 us -> none  [accumulate(): integral.astype(jnp.bfloat16).reshape(a_rows, c_rows, b_rows, col_count)]
    select_n x2 -> x0, other arithmetic: 7.87 us -> none  [the longest x1 7.86 us: accumulate(): masked = jnp.where(allowed, columns, jnp.zeros_like(columns))]
  transfers between devices with their start and end apart: 2 -> 0, of which waited for: 2 -> 0; matrix products, arithmetic and copies ran while one was open for 2% -> 0% of each run, Pallas kernels for 0% -> 0%
where the time goes in v1:
time: 66.1 us; the launch traced here: 66 us
  Pallas kernels  64.7 us (98%)
  local copies, waits for them, and re-layouts  1.28 us (2%)
    pallas_call x1, Pallas kernels, body(): pl.pallas_call(kernel, out_shape=jax.ShapeDtypeStruct((4, 256), F32), in_...  64.7 us

profile of v1, /device:TPU:1, one launch (start us, length us, event | category | flops | bytes accessed | tf_op | source)
XLA Modules:
  0.0 66.0 jit_solution(9733996390737632110)
XLA Ops:
  0.0 64.7 %ladder.1 = f32[4,256]{1,0:T(4,128)} custom-call(bf16[64,16,1024]{2,1,0:T(8,128)(2,1)} %bitcast.4, bf16[4,16,1024]{2,1,0:T(8,128)(2,1)} %bitcast.5, bf16[256,16,1024]{2,1,0:T(8,128)(2,1)} %amps.1, s32[1,64]{1,0:T(1,128)} %bitcast.7, s32[1,256]{1,0:T(1,128)} %bitcast.6), custom_call_target="tpu_custom_call" | custom-call | tf_op jit(solution)/shard_map/ladder/pallas_call | solution.py:430
  64.7 1.3 %copy.7 = f32[4,256]{1,0:T(4,128)} copy(f32[4,256]{1,0:T(4,128)} %ladder.1) | data formatting | bytes 8192

commit v2 on v1

--- a/solution.py
+++ b/solution.py
@@ -19,8 +19,6 @@
     ('z', 'X', 0, 1, 0, None),
     ('z', 'X', 0, 3, 0, None),
     ('z', 'X', 0, 2, 0, None),
-    ('z', 'X', 0, 0, 1, None),
-    ('z', 'X', 0, 0, 3, None),
     ('x+', 'X', 0, 0, 0, None),
     ('x-', 'X', 0, 0, 0, None),
     ('x+', 'X', 0, 1, 0, None),
@@ -29,6 +27,8 @@
     ('x-', 'X', 0, 3, 0, None),
     ('x+', 'X', 0, 2, 0, None),
     ('x-', 'X', 0, 2, 0, None),
+    ('x+', 'X', 1, 0, 0, None),
+    ('x-', 'X', 1, 0, 0, None),
     ('x+', 'X', 1, 1, 0, None),
     ('x-', 'X', 1, 1, 0, None),
     ('x+', 'X', 1, 3, 0, None),
@@ -51,8 +51,6 @@
     ('z', 'Y', 0, 0, 1, None),
     ('z', 'Y', 0, 0, 3, None),
     ('z', 'Y', 0, 0, 2, None),
-    ('z', 'Y', 0, 1, 0, None),
-    ('z', 'Y', 0, 3, 0, None),
     ('y+', 'Y', 0, 0, 0, None),
     ('y-', 'Y', 0, 0, 0, None),
     ('y+', 'Y', 0, 0, 1, None),
@@ -61,6 +59,8 @@
     ('y-', 'Y', 0, 0, 3, None),
     ('y+', 'Y', 0, 0, 2, None),
     ('y-', 'Y', 0, 0, 2, None),
+    ('y+', 'Y', 1, 0, 0, None),
+    ('y-', 'Y', 1, 0, 0, None),
     ('y+', 'Y', 1, 0, 1, None),
     ('y-', 'Y', 1, 0, 1, None),
     ('y+', 'Y', 1, 0, 3, None),
@@ -92,8 +92,9 @@
     ('c', 'X', 1, 2, None, None),
     ('c', 'Y', 1, 2, None, None),
 ]
+FIRST = [('send', 4), ('send', 33), ('send', 1), ('send', 32), ('send', 0)]
 BEFORE_LEFT = [
-    [],
+    [('send', 36), ('send', 8), ('send', 9), ('send', 40), ('send', 41)],
     [],
     [],
     [],
@@ -105,48 +106,26 @@
     [],
     [],
     [],
-    [],
-    [('barrier', 0), ('send', 1), ('send', 11), ('send', 36), ('send', 42), ('send', 32), ('send', 0), ('send', 10), ('send', 43), ('send', 33), ('send', 4)],
-    [],
-    [],
-    [],
-    [],
-    [],
-    [],
-    [],
+    [('wait', 4), ('send', 16), ('send', 17), ('wait', 33), ('send', 43), ('send', 42), ('send', 37), ('wait', 1), ('wait', 32), ('send', 34), ('send', 35), ('wait', 0), ('send', 45), ('send', 2), ('send', 38)],
+    [],
+    [],
+    [('send', 13), ('send', 10), ('send', 44)],
+    [],
+    [('wait', 36), ('wait', 9), ('wait', 41), ('wait', 8), ('wait', 40)],
+    [('send', 49), ('send', 5)],
+    [],
+    [('send', 24), ('send', 48), ('send', 11)],
     [],
 ]
-BEFORE_HALF = [
-    [
-        [('wait', 1), ('send', 5), ('send', 12), ('send', 3), ('send', 13), ('wait', 11), ('send', 8), ('wait', 36), ('wait', 42), ('send', 56), ('wait', 32), ('send', 47), ('send', 46), ('send', 34), ('send', 38), ('wait', 43), ('wait', 33), ('send', 44), ('send', 35), ('send', 45), ('wait', 4), ('wait', 0), ('send', 14), ('send', 15), ('wait', 10), ('send', 24), ('send', 37), ('send', 2), ('wait', 3), ('wait', 5), ('send', 19), ('send', 18), ('wait', 12), ('wait', 13), ('wait', 56), ('send', 9), ('wait', 34), ('wait', 47), ('wait', 35), ('send', 65), ('send', 49), ('send', 48), ('send', 26), ('wait', 8), ('send', 25), ('wait', 46), ('send', 60), ('send', 39), ('wait', 65), ('wait', 14), ('wait', 45), ('wait', 15), ('send', 28), ('wait', 38), ('send', 52), ('send', 53), ('wait', 44), ('send', 6), ('wait', 24), ('send', 64), ('wait', 19), ('send', 27), ('wait', 2), ('send', 17), ('wait', 49), ('send', 69), ('send', 16), ('send', 58), ('wait', 37), ('send', 51), ('send', 7), ('wait', 64)],
-        [('wait', 26), ('send', 68), ('wait', 60), ('wait', 27), ('send', 70), ('wait', 73), ('send', 62), ('wait', 39), ('send', 67), ('send', 55), ('wait', 51), ('send', 59), ('wait', 66), ('send', 41), ('wait', 28), ('send', 72), ('wait', 68), ('wait', 52), ('wait', 17), ('send', 54), ('wait', 70), ('wait', 6), ('send', 21), ('send', 20), ('wait', 67)],
-        [],
-        [('wait', 62), ('send', 77), ('wait', 71)],
-        [('wait', 63), ('wait', 22), ('wait', 76)],
-        [('wait', 74), ('wait', 31), ('send', 78)],
-        [],
-        [],
-    ],
-    [
-        [('wait', 18), ('wait', 25), ('wait', 69), ('wait', 48), ('send', 73), ('send', 50)],
-        [('wait', 72), ('wait', 16), ('send', 30), ('wait', 61), ('wait', 58)],
-        [('wait', 55), ('send', 63), ('wait', 50), ('wait', 40), ('send', 57), ('send', 71)],
-        [('wait', 41), ('wait', 30), ('send', 76), ('wait', 23), ('send', 31)],
-        [('wait', 29), ('send', 74), ('wait', 75)],
-        [('wait', 79)],
-        [],
-        [],
-    ],
-]
-BEFORE_FOLD = [
-    [('send', 40), ('wait', 9), ('send', 66), ('wait', 53), ('send', 61)],
-    [('wait', 7), ('send', 22), ('send', 23)],
-    [('wait', 21), ('send', 29), ('wait', 20), ('wait', 59)],
-    [('wait', 54), ('send', 75), ('wait', 77)],
-    [('wait', 57), ('send', 79)],
-    [('wait', 78)],
-    [],
-    [],
+BEFORE_CHUNK = [
+    [('wait', 16), ('wait', 17), ('wait', 43), ('send', 3), ('wait', 42), ('send', 6), ('wait', 37), ('wait', 34), ('send', 12), ('send', 25), ('wait', 35), ('send', 47), ('send', 46), ('send', 65), ('wait', 2), ('wait', 45), ('wait', 38), ('send', 39), ('wait', 10), ('send', 26), ('wait', 13), ('send', 51), ('send', 50), ('wait', 44), ('wait', 49), ('wait', 5), ('send', 19), ('wait', 24), ('send', 18), ('send', 64), ('wait', 11), ('send', 57), ('send', 58), ('wait', 3), ('send', 7), ('send', 15), ('wait', 48), ('wait', 6), ('wait', 12), ('send', 14), ('send', 21), ('wait', 25), ('send', 66), ('send', 52), ('send', 53), ('wait', 64), ('wait', 65)],
+    [('send', 20), ('send', 60), ('wait', 47), ('send', 69), ('wait', 46), ('send', 73), ('wait', 39), ('send', 67), ('send', 55), ('wait', 26), ('send', 68), ('wait', 19), ('send', 27), ('wait', 51), ('wait', 50), ('wait', 7), ('wait', 18), ('send', 28), ('send', 23), ('wait', 15), ('send', 59), ('send', 54), ('wait', 57), ('wait', 58), ('wait', 66), ('wait', 67)],
+    [('send', 62), ('send', 22), ('wait', 14), ('wait', 21), ('send', 29), ('wait', 53), ('send', 61), ('wait', 52), ('send', 56), ('send', 30), ('wait', 20), ('wait', 27), ('send', 70), ('wait', 55), ('send', 71), ('send', 63), ('wait', 60), ('wait', 68), ('wait', 69)],
+    [('wait', 28), ('send', 72), ('wait', 23), ('send', 31), ('wait', 59), ('wait', 54), ('send', 75), ('wait', 70), ('wait', 71)],
+    [('wait', 62), ('wait', 22), ('wait', 29), ('send', 74), ('wait', 61), ('wait', 72), ('wait', 73)],
+    [('wait', 56), ('send', 77), ('wait', 30), ('send', 76), ('wait', 63), ('send', 79), ('wait', 31), ('send', 78), ('wait', 74), ('wait', 75)],
+    [('wait', 76), ('wait', 77)],
+    [('wait', 78), ('wait', 79)],
 ]
 
 
@@ -227,7 +206,7 @@
     chol_a, chol_b, amps, virt, pair, out,
     held, left, amps_in, amps_c, mask, integral, acc,
     halves, plane_out, plane_in, column_out, column_in, left_in,
-    send_sems, recv_sems, load_sems, half_sems, plane_sems, column_sems,
+    heard_sems, send_sems, recv_sems, load_sems, half_sems, plane_sems, column_sems,
 ):
     at = Place()
     loads = [
@@ -240,11 +219,18 @@
     for load in loads:
         load.start()
     barrier = pltpu.get_barrier_semaphore()
-    peers = [at.neighbour("c")]
-    peers += [at.in_plane(lax.rem(at.xy + step, 16)) for step in range(1, 16)]
-    peers += [at.on_column(lax.rem(at.slab + step, 8)) for step in range(1, 8)]
+    up, down = (at.on_column(lax.rem(at.slab + step, 8)) for step in (1, 7))
+    peers = [at.neighbour(link) for link in ("c", "x+", "x-", "y+", "y-")] + [up, down]
     for peer in peers:
         pl.semaphore_signal(barrier, inc=1, device_id=peer, device_id_type=MESH)
+
+    def hear(count):
+        if count:
+            pl.semaphore_wait(heard_sems.at[count - 1, 0], 1)
+            pl.semaphore_wait(heard_sems.at[count - 1, 1], 1)
+        if count < 3:
+            pl.semaphore_signal(heard_sems.at[count, 0], inc=1, device_id=up, device_id_type=MESH)
+            pl.semaphore_signal(heard_sems.at[count, 1], inc=1, device_id=down, device_id_type=MESH)
 
     def move(kind, number):
         copy = transfer(at, held, send_sems, recv_sems, number, kind == "wait")
@@ -256,15 +242,21 @@
     def moves(table, step):
         for turn, entries in enumerate(table):
             if entries:
+                if isinstance(step, int):
+                    for kind, number in entries:
+                        move(kind, number)
+                    continue
 
                 @pl.when(step == turn)
                 def _():
                     for kind, number in entries:
-                        if kind == "barrier":
-                            loads[0].wait()
-                            pl.semaphore_wait(barrier, len(peers))
-                        else:
-                            move(kind, number)
+                        move(kind, number)
+
+    loads[0].wait()
+    pl.semaphore_wait(barrier, len(peers))
+    for kind, number in FIRST:
+        move(kind, number)
+    hear(0)
 
     def iota(shape, dim):
         return lax.broadcasted_iota(jnp.int32, shape, dim)
@@ -307,6 +299,12 @@
                 loads[2 + 2 * piece].wait()
                 loads[3 + 2 * piece].wait()
 
+        for turn in (1, 2):
+
+            @pl.when(group == 7 * turn)
+            def _():
+                hear(turn)
+
         moves(BEFORE_AMPS, group)
         rows = pl.ds(pl.multiple_of(group * 16, 16), 16)
         for chunk in range(CHUNKS):
@@ -321,25 +319,37 @@
             )
             amps_c[chunk, :, rows, :] = jnp.swapaxes(block, 0, 1) * mask[chunk, rows, :][None]
 
-    @pl.loop(0, CHUNKS)
-    def _(step):
+    def multiply(step):
         z, y = chunk_of(at, step)
         for half in range(2):
-            moves(BEFORE_HALF[half], step)
             vectors = held[2 * half : 2 * half + 2, z, y].reshape(256, 1024)
             block = lax.dot_general(
                 left[...].reshape(1024, 1024), vectors, NT, preferred_element_type=F32
             ).astype(BF16)
             for c in range(16):
                 for b in range(2):
-                    integral[(2 * half + b) * 64 : (2 * half + b + 1) * 64, c * 128 : (c + 1) * 128] = (
+                    integral[lax.rem(step, 2), pl.ds((2 * half + b) * 64, 64), pl.ds(c * 128, 128)] = (
                         block[c * 64 : (c + 1) * 64, b * 128 : (b + 1) * 128]
                     )
-        moves(BEFORE_FOLD, step)
+
+    def fold(step):
+        z, y = chunk_of(at, step)
         masked = jnp.concatenate([amps_c[z * 4 + y, c] for c in range(16)], 1)
         acc[...] += lax.dot_general(
-            masked, integral[...], NT, preferred_element_type=F32
+            masked, integral[lax.rem(step, 2)], NT, preferred_element_type=F32
         ).reshape(16, 2, 8, 256)
+
+    moves(BEFORE_CHUNK[:1], 0)
+    multiply(0)
+    hear(3)
+
+    @pl.loop(1, CHUNKS)
+    def _(step):
+        moves([[]] + BEFORE_CHUNK[1:], step)
+        fold(step - 1)
+        multiply(step)
+
+    fold(CHUNKS - 1)
 
     swap = pltpu.make_async_remote_copy(
         src_ref=acc.at[:, 1 - at.core],
@@ -438,7 +448,7 @@
             pltpu.VMEM((pairs, c_rows, virt), BF16),
             pltpu.VMEM((CHUNKS, c_rows, pairs, 128), BF16),
             pltpu.VMEM((CHUNKS, pairs, 128), BF16),
-            pltpu.VMEM((256, 2048), BF16),
+            pltpu.VMEM((2, 256, 2048), BF16),
             pltpu.VMEM((16, 2, 8, 256), F32),
             pltpu.VMEM((16, 8, 256), F32),
             pltpu.VMEM((16, 16, 128), BF16),
@@ -446,6 +456,7 @@
             pltpu.VMEM((16, 128), BF16),
             pltpu.VMEM((8, 16, 128), BF16),
             pltpu.VMEM((a_rows, c_rows, vec), BF16),
+            pltpu.SemaphoreType.REGULAR((3, 2)),
             dma((len(MOVES),)),
             dma((len(MOVES),)),
             dma((10,)),

time: 66.1 us -> 53.1 us (0.80)
  Pallas kernels: 64.7 us -> 51.6 us
    pallas_call x1, Pallas kernels: 64.7 us -> 51.6 us  [body(): pl.pallas_call(kernel, out_shape=jax.ShapeDtypeStruct((4, 256), F32), in_...]
where the time goes in v2:
time: 53.1 us; the launch traced here: 52.9 us
  Pallas kernels  51.6 us (97%)
  local copies, waits for them, and re-layouts  1.28 us (2%)
    pallas_call x1, Pallas kernels, body(): pl.pallas_call(kernel, out_shape=jax.ShapeDtypeStruct((4, 256), F32), in_...  51.6 us
    unnamed x1, local copies, waits for them, and re-layouts  1.28 us

profile of v2, /device:TPU:1, one launch (start us, length us, event | category | flops | bytes accessed | tf_op | source)
XLA Modules:
  0.0 52.9 jit_solution(18282495229136847460)
XLA Ops:
  0.0 51.6 %ladder.1 = f32[4,256]{1,0:T(4,128)} custom-call(bf16[64,16,1024]{2,1,0:T(8,128)(2,1)} %bitcast.4, bf16[4,16,1024]{2,1,0:T(8,128)(2,1)} %bitcast.5, bf16[256,16,1024]{2,1,0:T(8,128)(2,1)} %amps.1, s32[1,64]{1,0:T(1,128)} %bitcast.7, s32[1,256]{1,0:T(1,128)} %bitcast.6), custom_call_target="tpu_custom_call" | custom-call | tf_op jit(solution)/shard_map/ladder/pallas_call | solution.py:440
  51.7 1.3 %copy.7 = f32[4,256]{1,0:T(4,128)} copy(f32[4,256]{1,0:T(4,128)} %ladder.1) | data formatting | bytes 8192

commit v3 on v2

--- a/solution.py
+++ b/solution.py
@@ -21,27 +21,28 @@
     ('z', 'X', 0, 2, 0, None),
     ('x+', 'X', 0, 0, 0, None),
     ('x-', 'X', 0, 0, 0, None),
+    ('x+', 'X', 0, 0, 3, 0),
+    ('x-', 'X', 0, 0, 1, 1),
     ('x+', 'X', 0, 1, 0, None),
     ('x-', 'X', 0, 1, 0, None),
+    ('x+', 'X', 0, 1, 3, None),
     ('x+', 'X', 0, 3, 0, None),
     ('x-', 'X', 0, 3, 0, None),
+    ('x-', 'X', 0, 3, 1, None),
     ('x+', 'X', 0, 2, 0, None),
     ('x-', 'X', 0, 2, 0, None),
+    ('x+', 'X', 0, 2, 3, None),
     ('x+', 'X', 1, 0, 0, None),
     ('x-', 'X', 1, 0, 0, None),
+    ('x-', 'X', 1, 0, 1, None),
     ('x+', 'X', 1, 1, 0, None),
     ('x-', 'X', 1, 1, 0, None),
+    ('x+', 'X', 1, 1, 3, None),
     ('x+', 'X', 1, 3, 0, None),
     ('x-', 'X', 1, 3, 0, None),
+    ('x-', 'X', 1, 3, 1, None),
     ('x+', 'X', 1, 2, 0, None),
     ('x-', 'X', 1, 2, 0, None),
-    ('x+', 'X', 0, 0, 3, None),
-    ('x-', 'X', 1, 0, 1, None),
-    ('x+', 'X', 0, 1, 3, None),
-    ('x-', 'X', 1, 1, 1, None),
-    ('x+', 'X', 0, 3, 3, None),
-    ('x-', 'X', 1, 3, 1, None),
-    ('x+', 'X', 0, 2, 3, None),
     ('x-', 'X', 1, 2, 1, None),
     ('x+', 'Y', 0, 0, 0, None),
     ('x-', 'Y', 0, 0, 0, None),
@@ -53,38 +54,38 @@
     ('z', 'Y', 0, 0, 2, None),
     ('y+', 'Y', 0, 0, 0, None),
     ('y-', 'Y', 0, 0, 0, None),
+    ('y+', 'Y', 0, 3, 0, None),
     ('y+', 'Y', 0, 0, 1, None),
     ('y-', 'Y', 0, 0, 1, None),
+    ('y-', 'Y', 0, 1, 1, None),
     ('y+', 'Y', 0, 0, 3, None),
     ('y-', 'Y', 0, 0, 3, None),
+    ('y+', 'Y', 0, 3, 3, None),
     ('y+', 'Y', 0, 0, 2, None),
     ('y-', 'Y', 0, 0, 2, None),
+    ('y-', 'Y', 0, 1, 2, None),
     ('y+', 'Y', 1, 0, 0, None),
     ('y-', 'Y', 1, 0, 0, None),
+    ('y+', 'Y', 1, 3, 0, None),
     ('y+', 'Y', 1, 0, 1, None),
     ('y-', 'Y', 1, 0, 1, None),
+    ('y-', 'Y', 1, 1, 1, None),
     ('y+', 'Y', 1, 0, 3, None),
     ('y-', 'Y', 1, 0, 3, None),
+    ('y+', 'Y', 1, 3, 3, None),
     ('y+', 'Y', 1, 0, 2, None),
     ('y-', 'Y', 1, 0, 2, None),
-    ('y+', 'Y', 0, 3, 0, None),
-    ('y-', 'Y', 1, 1, 0, None),
-    ('y+', 'Y', 0, 3, 1, None),
-    ('y-', 'Y', 1, 1, 1, None),
-    ('y+', 'Y', 0, 3, 3, None),
-    ('y-', 'Y', 1, 1, 3, None),
-    ('y+', 'Y', 0, 3, 2, None),
     ('y-', 'Y', 1, 1, 2, None),
     ('c', 'X', 0, 0, None, None),
     ('c', 'Y', 0, 0, None, None),
+    ('c', 'X', 0, 1, None, None),
+    ('c', 'Y', 0, 1, None, None),
+    ('c', 'X', 0, 3, None, None),
+    ('c', 'Y', 0, 3, None, None),
     ('c', 'X', 1, 0, None, None),
     ('c', 'Y', 1, 0, None, None),
-    ('c', 'X', 0, 1, None, None),
-    ('c', 'Y', 0, 1, None, None),
     ('c', 'X', 1, 1, None, None),
     ('c', 'Y', 1, 1, None, None),
-    ('c', 'X', 0, 3, None, None),
-    ('c', 'Y', 0, 3, None, None),
     ('c', 'X', 1, 3, None, None),
     ('c', 'Y', 1, 3, None, None),
     ('c', 'X', 0, 2, None, None),
@@ -92,9 +93,10 @@
     ('c', 'X', 1, 2, None, None),
     ('c', 'Y', 1, 2, None, None),
 ]
-FIRST = [('send', 4), ('send', 33), ('send', 1), ('send', 32), ('send', 0)]
+ORDER = [(0, 0), (0, 1), (0, 3), (1, 0), (1, 1), (1, 3), (0, 2), (1, 2)]
+FIRST = [('send', 33), ('send', 34), ('send', 41), ('send', 1), ('send', 4), ('send', 8), ('send', 9), ('send', 0), ('send', 42), ('send', 37)]
 BEFORE_LEFT = [
-    [('send', 36), ('send', 8), ('send', 9), ('send', 40), ('send', 41)],
+    [],
     [],
     [],
     [],
@@ -105,27 +107,27 @@
     [],
     [],
     [],
-    [],
-    [('wait', 4), ('send', 16), ('send', 17), ('wait', 33), ('send', 43), ('send', 42), ('send', 37), ('wait', 1), ('wait', 32), ('send', 34), ('send', 35), ('wait', 0), ('send', 45), ('send', 2), ('send', 38)],
-    [],
-    [],
-    [('send', 13), ('send', 10), ('send', 44)],
-    [],
-    [('wait', 36), ('wait', 9), ('wait', 41), ('wait', 8), ('wait', 40)],
-    [('send', 49), ('send', 5)],
-    [],
-    [('send', 24), ('send', 48), ('send', 11)],
+    [('wait', 33), ('send', 35), ('send', 47), ('wait', 34), ('send', 36), ('send', 45), ('wait', 41), ('wait', 1), ('send', 12), ('send', 3), ('send', 5), ('send', 48), ('send', 39), ('wait', 4), ('send', 22)],
+    [],
+    [],
+    [],
+    [],
+    [('wait', 8), ('wait', 9), ('send', 11), ('wait', 0), ('send', 15), ('send', 16), ('send', 2), ('send', 6), ('send', 10), ('send', 13), ('send', 44), ('wait', 42), ('wait', 37)],
+    [],
+    [],
+    [('wait', 35), ('wait', 36), ('send', 50), ('send', 51), ('send', 40), ('send', 66), ('send', 54), ('send', 38)],
+    [],
     [],
 ]
 BEFORE_CHUNK = [
-    [('wait', 16), ('wait', 17), ('wait', 43), ('send', 3), ('wait', 42), ('send', 6), ('wait', 37), ('wait', 34), ('send', 12), ('send', 25), ('wait', 35), ('send', 47), ('send', 46), ('send', 65), ('wait', 2), ('wait', 45), ('wait', 38), ('send', 39), ('wait', 10), ('send', 26), ('wait', 13), ('send', 51), ('send', 50), ('wait', 44), ('wait', 49), ('wait', 5), ('send', 19), ('wait', 24), ('send', 18), ('send', 64), ('wait', 11), ('send', 57), ('send', 58), ('wait', 3), ('send', 7), ('send', 15), ('wait', 48), ('wait', 6), ('wait', 12), ('send', 14), ('send', 21), ('wait', 25), ('send', 66), ('send', 52), ('send', 53), ('wait', 64), ('wait', 65)],
-    [('send', 20), ('send', 60), ('wait', 47), ('send', 69), ('wait', 46), ('send', 73), ('wait', 39), ('send', 67), ('send', 55), ('wait', 26), ('send', 68), ('wait', 19), ('send', 27), ('wait', 51), ('wait', 50), ('wait', 7), ('wait', 18), ('send', 28), ('send', 23), ('wait', 15), ('send', 59), ('send', 54), ('wait', 57), ('wait', 58), ('wait', 66), ('wait', 67)],
-    [('send', 62), ('send', 22), ('wait', 14), ('wait', 21), ('send', 29), ('wait', 53), ('send', 61), ('wait', 52), ('send', 56), ('send', 30), ('wait', 20), ('wait', 27), ('send', 70), ('wait', 55), ('send', 71), ('send', 63), ('wait', 60), ('wait', 68), ('wait', 69)],
-    [('wait', 28), ('send', 72), ('wait', 23), ('send', 31), ('wait', 59), ('wait', 54), ('send', 75), ('wait', 70), ('wait', 71)],
-    [('wait', 62), ('wait', 22), ('wait', 29), ('send', 74), ('wait', 61), ('wait', 72), ('wait', 73)],
-    [('wait', 56), ('send', 77), ('wait', 30), ('send', 76), ('wait', 63), ('send', 79), ('wait', 31), ('send', 78), ('wait', 74), ('wait', 75)],
-    [('wait', 76), ('wait', 77)],
-    [('wait', 78), ('wait', 79)],
+    [('wait', 47), ('wait', 45), ('send', 46), ('wait', 5), ('wait', 12), ('send', 14), ('send', 24), ('send', 21), ('wait', 22), ('send', 23), ('wait', 3), ('wait', 2), ('send', 18), ('send', 7), ('wait', 11), ('wait', 39), ('send', 59), ('send', 60), ('send', 43), ('send', 53), ('wait', 15), ('wait', 48), ('wait', 44), ('wait', 10), ('send', 65), ('wait', 16), ('send', 17), ('wait', 6), ('send', 28), ('send', 25), ('wait', 51), ('send', 68), ('wait', 50), ('send', 70), ('wait', 65), ('wait', 66)],
+    [('wait', 14), ('wait', 13), ('send', 67), ('wait', 40), ('send', 63), ('wait', 54), ('wait', 59), ('wait', 24), ('send', 26), ('wait', 23), ('wait', 38), ('send', 56), ('send', 57), ('send', 72), ('send', 62), ('send', 52), ('send', 49), ('send', 61), ('wait', 46), ('wait', 43), ('wait', 21), ('send', 71), ('wait', 17), ('send', 69), ('wait', 7), ('send', 30), ('send', 31), ('send', 27), ('wait', 67), ('wait', 68)],
+    [('wait', 60), ('wait', 53), ('send', 55), ('wait', 18), ('send', 20), ('wait', 28), ('send', 29), ('send', 19), ('wait', 69), ('wait', 70)],
+    [('wait', 63), ('send', 64), ('wait', 56), ('wait', 26), ('wait', 25), ('send', 73), ('wait', 57), ('send', 58), ('send', 74), ('wait', 62), ('send', 76), ('wait', 71), ('wait', 72)],
+    [('wait', 30), ('wait', 31), ('send', 32), ('wait', 52), ('wait', 49), ('send', 78), ('wait', 27), ('wait', 29), ('send', 75), ('wait', 73), ('wait', 74)],
+    [('wait', 61), ('wait', 64), ('wait', 20), ('wait', 19), ('send', 77), ('wait', 75), ('wait', 76)],
+    [('wait', 55), ('wait', 58), ('send', 80), ('wait', 32), ('send', 79), ('wait', 77), ('wait', 78)],
+    [('wait', 79), ('wait', 80)],
 ]
 
 
@@ -197,9 +199,11 @@
 
 
 def chunk_of(at, step):
-    turn = lax.div(step, 2)
-    dy = turn + lax.div(turn, 2) - 2 * lax.div(turn, 3)
-    return lax.rem(at.z + lax.rem(step, 2), 2), lax.rem(at.y + dy, 4)
+    dz, dy = 0, 0
+    for turn, (above, beside) in enumerate(ORDER):
+        dz = jnp.where(step == turn, above, dz)
+        dy = jnp.where(step == turn, beside, dy)
+    return lax.rem(at.z + dz, 2), lax.rem(at.y + dy, 4)
 
 
 def kernel(
@@ -369,8 +373,10 @@
     pairs = jnp.dot(pairs, turn, preferred_element_type=F32).reshape(16, 8, 256)
     plane_out[...] = jnp.concatenate([pairs[:, :, :128], pairs[:, :, 128:]], 1).astype(BF16)
     copies = []
-    for step in range(1, 16):
-        other = lax.rem(at.xy + step, 16)
+    far_first = [(dy, dx) for dy in (2, 1, 3, 0) for dx in (2, 1, 3, 0) if dy or dx]
+    far_first.sort(key=lambda d: min(d[0], 4 - d[0]) + min(d[1], 4 - d[1]), reverse=True)
+    others = [lax.rem(at.y + dy, 4) * 4 + lax.rem(at.x + dx, 4) for dy, dx in far_first]
+    for other in others:
         copies.append(
             pltpu.make_async_remote_copy(
                 src_ref=plane_out.at[other],
@@ -383,8 +389,7 @@
         )
         copies[-1].start()
     total = plane_out[at.xy].astype(F32)
-    for step in range(1, 16):
-        other = lax.rem(at.xy + step, 16)
+    for other in others:
         pltpu.make_async_remote_copy(
             src_ref=plane_out.at[other],
             dst_ref=plane_in.at[other],
@@ -395,8 +400,8 @@
         ).wait_recv()
         total += plane_in[other].astype(F32)
     column_out[...] = total.astype(BF16)
-    for step in range(1, 8):
-        other = lax.rem(at.slab + step, 8)
+    others = [lax.rem(at.slab + step, 8) for step in (4, 3, 5, 2, 6, 1, 7)]
+    for other in others:
         copies.append(
             pltpu.make_async_remote_copy(
                 src_ref=column_out,
@@ -409,8 +414,7 @@
         )
         copies[-1].start()
     total = column_out[...].astype(F32)
-    for step in range(1, 8):
-        other = lax.rem(at.slab + step, 8)
+    for other in others:
         pltpu.make_async_remote_copy(
             src_ref=column_out,
             dst_ref=column_in.at[other],

time: 53.1 us -> 51.8 us (0.976)
  Pallas kernels: 51.6 us -> 50.4 us
    pallas_call x1, Pallas kernels: 51.6 us -> 50.4 us  [body(): pl.pallas_call(kernel, out_shape=jax.ShapeDtypeStruct((4, 256), F32), in_...]
where the time goes in v3:
time: 51.8 us; the launch traced here: 51.7 us
  Pallas kernels  50.4 us (97%)
  local copies, waits for them, and re-layouts  1.28 us (2%)
    pallas_call x1, Pallas kernels, body(): pl.pallas_call(kernel, out_shape=jax.ShapeDtypeStruct((4, 256), F32), in_...  50.4 us
    unnamed x1, local copies, waits for them, and re-layouts  1.28 us

profile of v3, /device:TPU:1, one launch (start us, length us, event | category | flops | bytes accessed | tf_op | source)
XLA Modules:
  0.0 51.7 jit_solution(16206977404086405188)
XLA Ops:
  0.0 50.4 %ladder.1 = f32[4,256]{1,0:T(4,128)} custom-call(bf16[64,16,1024]{2,1,0:T(8,128)(2,1)} %bitcast.4, bf16[4,16,1024]{2,1,0:T(8,128)(2,1)} %bitcast.5, bf16[256,16,1024]{2,1,0:T(8,128)(2,1)} %amps.1, s32[1,64]{1,0:T(1,128)} %bitcast.7, s32[1,256]{1,0:T(1,128)} %bitcast.6), custom_call_target="tpu_custom_call" | custom-call | tf_op jit(solution)/shard_map/ladder/pallas_call | solution.py:444
  50.4 1.3 %copy.7 = f32[4,256]{1,0:T(4,128)} copy(f32[4,256]{1,0:T(4,128)} %ladder.1) | data formatting | bytes 8192

commit v4 on v3

--- a/solution.py
+++ b/solution.py
@@ -364,13 +364,8 @@
         device_id_type=MESH,
     )
     swap.start()
-    turn = (
-        (lax.rem(iota((256, 256), 0), 64) == lax.div(iota((256, 256), 1), 4))
-        & (lax.div(iota((256, 256), 0), 64) == lax.rem(iota((256, 256), 1), 4))
-    ).astype(F32).astype(BF16)
     swap.wait_recv()
-    pairs = (acc[:, at.core] + halves[...]).reshape(128, 256).astype(BF16)
-    pairs = jnp.dot(pairs, turn, preferred_element_type=F32).reshape(16, 8, 256)
+    pairs = acc[:, at.core] + halves[...]
     plane_out[...] = jnp.concatenate([pairs[:, :, :128], pairs[:, :, 128:]], 1).astype(BF16)
     copies = []
     far_first = [(dy, dx) for dy in (2, 1, 3, 0) for dx in (2, 1, 3, 0) if dy or dx]
@@ -441,7 +436,7 @@
     anywhere = pl.BlockSpec(memory_space=pl.ANY)
     inside = pl.BlockSpec(memory_space=pltpu.VMEM)
     dma = pltpu.SemaphoreType.DMA
-    return pl.pallas_call(
+    sums = pl.pallas_call(
         kernel,
         out_shape=jax.ShapeDtypeStruct((4, 256), F32),
         in_specs=[anywhere, anywhere, anywhere, inside, inside],
@@ -479,6 +474,7 @@
         virt_irrep.reshape(1, -1),
         pair_irrep.reshape(1, -1),
     )
+    return sums.reshape(4, b_rows, a_rows).transpose(0, 2, 1).reshape(4, a_rows * b_rows)
 
 
 def solution(mesh):

time: 51.8 us -> 51.9 us (level)
    reshape x0 -> x3, local copies, waits for them, and re-layouts: none -> 1.6 us  [body(): sums.reshape(4, b_rows, a_rows).transpose(0, 2, 1)]
    unnamed x1 -> x0, local copies, waits for them, and re-layouts: 1.28 us -> none
where the time goes in v4:
time: 51.9 us; the launch traced here: 51.8 us
  Pallas kernels  50.2 us (97%)
  local copies, waits for them, and re-layouts  1.6 us (3%)
    pallas_call x1, Pallas kernels, body(): pl.pallas_call(kernel, out_shape=jax.ShapeDtypeStruct((4, 256), F32), in_...  50.2 us
    reshape x3, local copies, waits for them, and re-layouts, body(): sums.reshape(4, b_rows, a_rows).transpose(0, 2, 1)  1.6 us

profile of v4, /device:TPU:1, one launch (start us, length us, event | category | flops | bytes accessed | tf_op | source)
XLA Modules:
  0.0 51.8 jit_solution(12951554147659898595)
XLA Ops:
  0.0 50.2 %ladder.1 = f32[4,256]{1,0:T(4,128)} custom-call(bf16[64,16,1024]{2,1,0:T(8,128)(2,1)} %bitcast.5, bf16[4,16,1024]{2,1,0:T(8,128)(2,1)} %bitcast.7, bf16[256,16,1024]{2,1,0:T(8,128)(2,1)} %amps.1, s32[1,64]{1,0:T(1,128)} %bitcast.9, s32[1,256]{1,0:T(1,128)} %bitcast.8), custom_call_target="tpu_custom_call" | custom-call | tf_op jit(solution)/shard_map/ladder/pallas_call | solution.py:439
  50.2 0.8 %reshape.14 = f32[4,4,64]{2,1,0:T(4,128)S(1)} reshape(f32[4,256]{1,0:T(4,128)} %ladder.1) | data formatting | bytes 8192 | tf_op jit(solution)/shard_map/reshape | solution.py:477
  51.0 0.1 copy.7
  51.1 0.7 %reshape.15 = f32[4,256]{1,0:T(4,128)} reshape(f32[4,64,4]{2,1,0:T(8,128)S(1)} %bitcast.6) | data formatting | bytes 8192 | tf_op jit(solution)/shard_map/reshape | solution.py:477
